TPU v7x, 256 devices: a whole 4x4x8 slice. The times are simulated.
256 devices in a mesh: section: 2 (over core), seq: 16 (over z, x_hi), vocab: 8 (over y, x_lo).
Axes of the slice: x: 4 (x_hi: 2, x_lo: 2; x = x_hi * 2 + x_lo), y: 4, z: 8, core: 2. Of those that a mesh axis runs over, the one named last changes fastest.
Arguments:
- hidden: bfloat16 [2, 2048, 4096], P(None, 'seq'), may hold values from -8 to 8
- head_weight: bfloat16 [4096, 20480], P('seq', ('section', 'vocab')), may hold values from -1 to 1
- teacher_logits: bfloat16 [2, 2048, 20480], P(None, 'seq', ('section', 'vocab')), may hold values from -300 to 300
- targets: int32 [2, 2048], P(None, 'seq'), may hold values from 0 to 20479
- span_inputs: bfloat16 [2, 2, 2, 2048, 4096], P('section', None, None, 'seq', 'vocab'), may hold values from -6 to 6
- span_gains: float32 [2, 2, 4096], P('section', None, 'vocab'), may hold values from 0.5 to 1.5
- span_weights: bfloat16 [2, 2, 32, 128, 128], P('section', None, 'vocab'), may hold values from -0.625 to 0.625
Outputs:
- input_grads: bfloat16 [2, 2, 2, 2048, 4096], P('section', None, None, 'seq', 'vocab')
- loss: float32 [], replicated
All inputs are finite; a program needn't handle non-finite values.
Results may differ from a plain program's by a relative error of at most 0.0069.
Values may be sent and summed in bfloat16 or wider, within the bound.
A program may use at most 64 MiB of HBM per device.

v0:
```python
import functools

import jax
import jax.numpy as jnp
from jax import lax
from jax.experimental import pallas as pl
from jax.experimental.pallas import tpu as pltpu
from jax.sharding import PartitionSpec as P

MESH = pl.DeviceIdType.MESH
F32 = jnp.float32
BF16 = jnp.bfloat16
LOSS_SCALE = 16
CE_WEIGHT = 0.5
EPS = 1e-06
HEAD = 128
SPAN_AT = ((0, 0), (1, 0), (1, 1), (0, 1))


def to_rows(columns, height):
    count = columns[0].shape[0]
    lane = lax.broadcasted_iota(jnp.int32, (count, 128), 1)
    wide = jnp.zeros((count, 128), F32)
    for i, column in enumerate(columns):
        wide = jnp.where(lane == i, column, wide)
    return wide.T[:height]


def to_columns(rows):
    height, count = rows.shape
    return jnp.concatenate([rows, jnp.zeros((128 - height, count), F32)], axis=0).T


def heads_dot(left, weights, transposed):
    dims = (((1,), (1,)), ((), ())) if transposed else (((1,), (0,)), ((), ()))
    parts = []
    for h in range(weights.shape[0]):
        parts.append(
            lax.dot_general(left[:, h * HEAD : (h + 1) * HEAD], weights[h], dims, preferred_element_type=F32)
        )
    return jnp.concatenate(parts, axis=1)


def kernel(
    nz, nv,
    hidden, head, teacher, targets, xin, gains, wspan,
    out, loss_ref,
    wbuf, hid, tea, tgt, logits, texp, dlog, stats, snd_x, rcv_x, snd_y, rcv_y, two_x, end_x, two_y, end_y, xs, gs, ws, branch,
    sq, dots, lsend, lrecv, ys,
    loc_sem, zs_sem, zr_sem, ds_sem, dr_sem, ms_sem, mr_sem, sts_sem, str_sem, xs_sem, xr_sem, ys_sem, yr_sem,
    exs_sem, exr_sem, eys_sem, eyr_sem,    sqs_sem, sqr_sem, dos_sem, dor_sem, ls_sem, lr_sem, os_sem, or_sem,
):
    core = lax.axis_index("section")
    seq = lax.axis_index("seq")
    voc = lax.axis_index("vocab")
    z, xh = seq // 2, seq % 2
    xl = voc % 2
    other = 1 - core
    half = nz // 2
    tok, width = hid.shape[1], hid.shape[2]
    rows, cols = head.shape[0], wbuf.shape[2]
    slice_width = xs.shape[3]
    plane = 2 * nv
    me = xh * nv + voc

    def at(c, zz, hh, v):
        return (c, zz * 2 + hh, v)

    def plane_peer(index):
        return at(core, z, index // nv, index % nv)

    mate = at(other, z, xh, voc)
    partner = at(core, z, 1 - xh, voc)
    partner_mate = at(other, z, 1 - xh, voc)
    near = at(core, z, 1 - xh, voc + 1 - 2 * xl)
    right = at(core, (z + 1) % nz, xh, voc)
    left = at(core, (z + nz - 1) % nz, xh, voc)
    far = []
    bit = 1
    while bit < nz:
        far.append(at(core, z + bit - 2 * bit * ((z // bit) % 2), xh, voc))
        bit *= 2

    barrier = pltpu.get_barrier_semaphore()
    direct = [mate, partner_mate, right, left] + far[1:]
    for peer in direct:
        pl.semaphore_signal(barrier, inc=1, device_id=peer, device_id_type=MESH)

    def greet(i, carry):
        pl.semaphore_signal(barrier, inc=1, device_id=plane_peer((me + i) % plane), device_id_type=MESH)
        return carry

    lax.fori_loop(1, plane, greet, 0)
    pl.semaphore_wait(barrier, len(direct) + plane - 1)

    def remote(src, dst, send, recv, peer):
        return pltpu.make_async_remote_copy(
            src_ref=src, dst_ref=dst, send_sem=send, recv_sem=recv, device_id=peer, device_id_type=MESH
        )

    sent = []

    def begin(copy):
        copy.start()
        sent.append(copy)

    part_rows = rows // 2

    def part_at(section, delta, part):
        zz = lax.rem(z + delta + nz, nz)
        hh = xh if part < 2 else 1 - xh
        start = (zz * 2 + hh) * rows + (part % 2) * part_rows
        return wbuf.at[section, pl.ds(pl.multiple_of(start, part_rows), part_rows), :]

    def own_columns(hh):
        return pl.ds(pl.multiple_of(hh * cols, cols), cols)

    own_block = head.at[:, own_columns(xh)]

    def own_part(part, hh):
        return head.at[pl.ds(part * part_rows, part_rows), own_columns(hh)]

    ring_parts = [
        [(k, part) for k in range(1, half) for part in range(4)] + [(half, 2 * way), (half, 2 * way + 1)]
        for way in (0, 1)
    ]
    ring_count = len(ring_parts[0])
    ring_copies = [[], []]

    def ring_send(way, i):
        k, part = ring_parts[way][i]
        slot = part_at(core, -(k - 1) if way == 0 else k - 1, part)
        src = own_part(part, xh) if k == 1 and part < 2 else slot
        if k > 1:
            ring_wait(way, ring_parts[way].index((k - 1, part)))
        if i >= 2:
            ring_copies[way][i - 2].wait_send()
        copy = remote(src, slot, zs_sem.at[way, i], zr_sem.at[way, i], right if way == 0 else left)
        copy.start()
        ring_copies[way].append(copy)

    arrived = [0, 0]

    def ring_wait(way, i):
        while arrived[way] <= i:
            j = arrived[way]
            k, part = ring_parts[way][j]
            delta = -k if way == 0 else k
            slot = part_at(core, delta, part)
            remote(slot, slot, zs_sem.at[way, j], zr_sem.at[way, j], right).wait_recv()
            mate_send(delta, part)
            arrived[way] += 1

    def mate_send(delta, part):
        slot = part_at(core, delta, part)
        src = own_part(part, xh) if delta == 0 and part < 2 else slot
        i = (delta % nz) * 4 + part
        begin(remote(src, slot, ds_sem.at[i], dr_sem.at[i], mate))

    def mate_wait(delta, part):
        slot = part_at(other, delta, part)
        i = (delta % nz) * 4 + part
        remote(slot, slot, ds_sem.at[i], dr_sem.at[i], mate).wait_recv()

    def partner_send(part):
        slot = part_at(core, 0, part)
        copy = remote(own_part(part, 1 - xh), slot, ms_sem.at[9 * part], mr_sem.at[9 * part], partner)
        copy.start()
        return copy

    def partner_wait(part):
        slot = part_at(core, 0, part + 2)
        remote(slot, slot, ms_sem.at[9 * part], mr_sem.at[9 * part], partner).wait_recv()
        mate_send(0, part + 2)

    my_rows = wbuf.at[core, pl.ds(pl.multiple_of(seq * rows, rows), rows), :]
    first = partner_send(0)
    for i in (0, 1):
        for way in (0, 1):
            ring_send(way, i)
        mate_send(0, i)

    local = [
        pltpu.make_async_copy(own_block, my_rows, loc_sem.at[0]),
        pltpu.make_async_copy(xin.at[0, :, core], xs.at[core], loc_sem.at[1]),
        pltpu.make_async_copy(gains.at[0], gs.at[core], loc_sem.at[2]),
        pltpu.make_async_copy(wspan.at[0], ws.at[core], loc_sem.at[3]),
        pltpu.make_async_copy(hidden.at[core], hid.at[xh], loc_sem.at[4]),
        pltpu.make_async_copy(teacher.at[core, :, own_columns(xh)], tea.at[core, xh], loc_sem.at[5]),
        pltpu.make_async_copy(targets, tgt.at[xh], loc_sem.at[6]),
    ]
    for copy in local:
        copy.start()
    begin(remote(xin.at[0, :, other], xs.at[core], ms_sem.at[1], mr_sem.at[1], mate))
    begin(remote(gains.at[0], gs.at[core], ms_sem.at[2], mr_sem.at[2], mate))
    begin(remote(wspan.at[0], ws.at[core], ms_sem.at[3], mr_sem.at[3], mate))
    begin(remote(teacher.at[other, :, own_columns(xh)], tea.at[core, xh], ms_sem.at[4], mr_sem.at[4], mate))

    first.wait_send()
    second = partner_send(1)
    partner_wait(0)
    for way in (0, 1):
        ring_send(way, 2)
    second.wait_send()
    begin(remote(hidden.at[core], hid.at[xh], ms_sem.at[5], mr_sem.at[5], near))
    begin(remote(targets, tgt.at[xh], ms_sem.at[6], mr_sem.at[6], partner))
    begin(remote(teacher.at[core, :, own_columns(1 - xh)], tea.at[core, xh], ms_sem.at[7], mr_sem.at[7], partner))
    begin(
        remote(teacher.at[other, :, own_columns(1 - xh)], tea.at[core, xh], ms_sem.at[8], mr_sem.at[8], partner_mate)
    )

    for copy in local:
        copy.wait()
    remote(xs.at[other], xs.at[other], ms_sem.at[1], mr_sem.at[1], mate).wait_recv()
    remote(gs.at[other], gs.at[other], ms_sem.at[2], mr_sem.at[2], mate).wait_recv()
    remote(ws.at[other], ws.at[other], ms_sem.at[3], mr_sem.at[3], mate).wait_recv()

    def saved(c):
        return xs[SPAN_AT[c]].astype(F32)

    def gain(c):
        section, slot_index = SPAN_AT[c]
        return gs[section, slot_index : slot_index + 1, :]

    def exchange(buf, send_sems, recv_sems):
        def send(i, carry):
            peer = at(core, z, xh, (voc + i) % nv)
            remote(buf.at[voc], buf.at[voc], send_sems.at[i], recv_sems.at[i], peer).start()
            return carry

        lax.fori_loop(1, nv, send, 0)

    def exchange_wait(buf, send_sems, recv_sems):
        def wait(i, carry):
            src = (voc + nv - i) % nv
            remote(buf.at[src], buf.at[src], send_sems.at[i], recv_sems.at[i], mate).wait_recv()
            remote(buf.at[voc], buf.at[voc], send_sems.at[i], recv_sems.at[i], mate).wait_send()
            return carry

        lax.fori_loop(1, nv, wait, 0)
        total = buf[0]
        for i in range(1, nv):
            total = total + buf[i]
        return total

    squares = []
    for c in range(4):
        value = saved(c)
        squares.append(jnp.sum(value * value, axis=1, keepdims=True))
    sq[voc] = to_rows(squares, 8)
    exchange(sq, sqs_sem, sqr_sem)
    for c in range(4):
        scaled = (saved(c) * gain(c)).astype(BF16)
        branch[c] = heads_dot(scaled, ws[SPAN_AT[c]], False)

    def multiply(delta, first=False):
        for part in range(4):
            mate_wait(delta, part)
        zz = lax.rem(z + delta + nz, nz)
        span = pl.ds(pl.multiple_of(zz * 2 * rows, 2 * rows), 2 * rows)
        left_part = hid[:, :, span].reshape(2 * tok, 2 * rows)
        for s in (0, 1):
            product = jnp.dot(left_part, wbuf[s, span, :], preferred_element_type=F32)
            if first:
                logits[s] = product
            else:
                logits[s] += product

    def hidden_wait():
        slot = hid.at[1 - xh]
        remote(slot, slot, ms_sem.at[5], mr_sem.at[5], near).wait_recv()

    def span_ready():
        total = to_columns(exchange_wait(sq, sqs_sem, sqr_sem))
        inv = [lax.rsqrt(total[:, c : c + 1] / width + EPS) for c in range(4)]

        def lift(c, value):
            grad = heads_dot(value.astype(BF16), ws[SPAN_AT[c]], True)
            return value + inv[c] * gain(c) * grad

        def inner(c, value):
            return jnp.sum(value * branch[c], axis=1, keepdims=True)

        u3 = saved(3) * inv[3] ** 3
        e32 = inner(2, u3)
        v = lift(2, u3)
        e31 = inner(1, v)
        v = lift(1, v)
        e30 = inner(0, v)
        u2 = saved(2) * inv[2] ** 3
        e21 = inner(1, u2)
        e20 = inner(0, lift(1, u2))
        e10 = inner(0, saved(1) * inv[1] ** 3)
        return inv, lift, inner, [e32, e31, e30, e21, e20, e10]

    def teacher_ready():
        pairs = ((other, xh, 4, mate), (core, 1 - xh, 7, partner), (other, 1 - xh, 8, partner_mate))
        for s, hh, i, peer in pairs:
            slot = tea.at[s, hh]
            remote(slot, slot, ms_sem.at[i], mr_sem.at[i], peer).wait_recv()
        slot = tgt.at[1 - xh]
        remote(slot, slot, ms_sem.at[6], mr_sem.at[6], partner).wait_recv()
        values = [tea[s].reshape(2 * tok, cols).astype(F32) for s in (0, 1)]
        top = jnp.max(jnp.maximum(values[0], values[1]), axis=1, keepdims=True)
        total = jnp.zeros((2 * tok, 1), F32)
        for s in (0, 1):
            value = jnp.exp(values[s] - top)
            texp[s] = value
            total += jnp.sum(value, axis=1, keepdims=True)
        return top, total

    partner_wait(1)
    for way in (0, 1):
        ring_send(way, 3)
    for i in range(4, ring_count):
        for way in (0, 1):
            ring_send(way, i)
        if i == 5:
            inv, lift, inner, cross_spans = span_ready()
    teacher_top, teacher_total = teacher_ready()
    hidden_wait()
    multiply(0, first=True)
    for i in range(ring_count - 4, ring_count):
        for way in (0, 1):
            ring_wait(way, i)
        if i == ring_count - 3:
            for d in range(1, half):
                multiply(-d)
                multiply(d)
    multiply(half)

    def target_column():
        parts = []
        for hh in (0, 1):
            row = jnp.where(core == 0, tgt[hh, 0:1, :], tgt[hh, 1:2, :])
            parts.append(jnp.broadcast_to(row, (128, tok)).T[:, 0:1])
        return jnp.concatenate(parts, axis=0)

    wanted = target_column()

    def hit(s):
        start = (s * nv + voc) * 2 * cols + xh * cols
        return wanted - start == lax.broadcasted_iota(jnp.int32, (2 * tok, cols), 1)

    student_top = jnp.max(jnp.maximum(logits[0], logits[1]), axis=1, keepdims=True)
    student_total = jnp.zeros((2 * tok, 1), F32)
    cross = jnp.zeros((2 * tok, 1), F32)
    target_logit = jnp.zeros((2 * tok, 1), F32)
    for s in (0, 1):
        value = logits[s]
        cross += jnp.sum(texp[s] * (tea[s].reshape(2 * tok, cols).astype(F32) - value), axis=1, keepdims=True)
        target_logit += jnp.sum(jnp.where(hit(s), value, 0.0), axis=1, keepdims=True)
        value = jnp.exp(value - student_top)
        logits[s] = value
        student_total += jnp.sum(value, axis=1, keepdims=True)
    stats[me] = to_rows([student_top, student_total, teacher_top, teacher_total, cross, target_logit], 8)

    def stats_send(i, carry):
        peer = plane_peer((me + i) % plane)
        remote(stats.at[me], stats.at[me], sts_sem.at[i], str_sem.at[i], peer).start()
        return carry

    def stats_wait(i, carry):
        src = (me + plane - i) % plane
        remote(stats.at[src], stats.at[src], sts_sem.at[i], str_sem.at[i], mate).wait_recv()
        remote(stats.at[me], stats.at[me], sts_sem.at[i], str_sem.at[i], mate).wait_send()
        return carry

    lax.fori_loop(1, plane, stats_send, 0)
    lax.fori_loop(1, plane, stats_wait, 0)
    top_s, top_t = stats[0, 0:1, :], stats[0, 2:3, :]
    for i in range(1, plane):
        top_s = jnp.maximum(top_s, stats[i, 0:1, :])
        top_t = jnp.maximum(top_t, stats[i, 2:3, :])
    sum_s, sum_t, sum_x, sum_l = (jnp.zeros_like(top_s) for _ in range(4))
    for i in range(plane):
        part = stats[i]
        sum_s += part[1:2] * jnp.exp(part[0:1] - top_s)
        factor = jnp.exp(part[2:3] - top_t)
        sum_t += part[3:4] * factor
        sum_x += part[4:5] * factor
        sum_l += part[5:6]
    lse_s = top_s + jnp.log(sum_s)
    lse_t = top_t + jnp.log(sum_t)
    terms = sum_x / sum_t - lse_t + lse_s + CE_WEIGHT * (lse_s - sum_l)
    scales = to_columns(jnp.concatenate([lse_s, lse_t], axis=0))
    student_scale = jnp.exp(student_top - scales[:, 0:1])
    teacher_scale = jnp.exp(teacher_top - scales[:, 1:2])

    loss_peers = [mate] + far
    lsend[0] = jnp.broadcast_to(jnp.sum(terms, axis=1, keepdims=True), (8, 128))

    def loss_send(level):
        begin(remote(lsend.at[level], lrecv.at[level], ls_sem.at[level], lr_sem.at[level], loss_peers[level]))

    def loss_wait(level):
        slot = lrecv.at[level]
        remote(slot, slot, ls_sem.at[level], lr_sem.at[level], mate).wait_recv()
        return lsend[level] + lrecv[level]

    loss_send(0)

    for s in (0, 1):
        value = (1.0 + CE_WEIGHT) * (logits[s] * student_scale) - texp[s] * teacher_scale
        value = value - jnp.where(hit(s), CE_WEIGHT, 0.0)
        dlog[s] = (LOSS_SCALE * value).astype(BF16)

    half_tok = tok // 2
    ny = nv // 2
    xi, yi = xh * 2 + xl, voc // 2
    nt = (((1,), (1,)), ((), ()))

    def in_plane(x, y):
        return at(core, z, x // 2, y * 2 + x % 2)

    def slice_turn(i, carry):
        oy = (i // 2 + 1) % ny
        y = (yi + oy) % ny
        lo = (xl + 1 + i) % 2
        v = y * 2 + lo
        span = pl.ds(pl.multiple_of(v * slice_width, slice_width), slice_width)
        part = lax.dot_general(dlog[0], wbuf[0, span, :], nt, preferred_element_type=F32)
        part += lax.dot_general(dlog[1], wbuf[1, span, :], nt, preferred_element_type=F32)
        part = part.astype(BF16)
        for hh in (0, 1):
            x = hh * 2 + lo
            ox = (x - xi + 4) % 4
            snd_x[x, y] = part[hh * tok : hh * tok + half_tok]
            snd_y[y, x] = part[hh * tok + half_tok : (hh + 1) * tok]

            @pl.when(ox != 0)
            def _():
                remote(
                    snd_x.at[x, y], rcv_x.at[xi, y], xs_sem.at[ox, oy], xr_sem.at[ox, oy], in_plane(x, yi)
                ).start()

            @pl.when(oy != 0)
            def _():
                remote(
                    snd_y.at[y, x], rcv_y.at[yi, x], ys_sem.at[oy, ox], yr_sem.at[oy, ox], in_plane(xi, y)
                ).start()

        return carry

    lax.fori_loop(0, nv, slice_turn, 0)
    if len(loss_peers) > 1:
        lsend[1] = loss_wait(0)
        loss_send(1)

    def sum_x(oy):
        y = (yi + oy) % ny
        total = snd_x[xi, y].astype(F32)
        for ox in range(1, 4):
            slot = rcv_x.at[(xi + 4 - ox) % 4, y]
            remote(slot, slot, xs_sem.at[ox, oy], xr_sem.at[ox, oy], mate).wait_recv()
            total = total + slot[...].astype(F32)
        return total

    def sum_y(ox):
        x = (xi + ox) % 4
        total = snd_y[yi, x].astype(F32)
        for oy in range(1, ny):
            slot = rcv_y.at[(yi + ny - oy) % ny, x]
            remote(slot, slot, ys_sem.at[oy, ox], yr_sem.at[oy, ox], mate).wait_recv()
            total = total + slot[...].astype(F32)
        return total

    for oy in range(1, ny):
        two_y[oy] = sum_x(oy).astype(BF16)
        begin(remote(two_y.at[oy], end_y.at[oy], eys_sem.at[oy], eyr_sem.at[oy], in_plane(xi, (yi + oy) % ny)))
    for ox in range(1, 4):
        two_x[ox] = sum_y(ox).astype(BF16)
        begin(remote(two_x.at[ox], end_x.at[ox], exs_sem.at[ox], exr_sem.at[ox], in_plane((xi + ox) % 4, yi)))
    first_half, second_half = sum_x(0), sum_y(0)
    for oy in range(1, ny):
        remote(end_y.at[oy], end_y.at[oy], eys_sem.at[oy], eyr_sem.at[oy], mate).wait_recv()
        first_half = first_half + end_y[oy].astype(F32)
    for ox in range(1, 4):
        remote(end_x.at[ox], end_x.at[ox], exs_sem.at[ox], exr_sem.at[ox], mate).wait_recv()
        second_half = second_half + end_x[ox].astype(F32)
    cotangent = jnp.concatenate([first_half.astype(BF16), second_half.astype(BF16)], axis=0)

    def slice_sent(i, carry):
        oy, ox = i // 4, i % 4

        @pl.when(ox != 0)
        def _():
            x, y = (xi + ox) % 4, (yi + oy) % ny
            remote(snd_x.at[x, y], rcv_x.at[xi, y], xs_sem.at[ox, oy], xr_sem.at[ox, oy], mate).wait_send()

        @pl.when(oy != 0)
        def _():
            x, y = (xi + ox) % 4, (yi + oy) % ny
            remote(snd_y.at[y, x], rcv_y.at[yi, x], ys_sem.at[oy, ox], yr_sem.at[oy, ox], mate).wait_send()

        return carry

    lax.fori_loop(0, 4 * ny, slice_sent, 0)

    value = cotangent.astype(F32)
    products = [inner(3, value)]
    for c in (3, 2, 1):
        value = lift(c, value)
        products.append(inner(c - 1, value))
    dots[voc] = to_rows(products + cross_spans, 16)
    exchange(dots, dos_sem, dor_sem)
    for level in range(2, len(loss_peers)):
        lsend[level] = loss_wait(level - 1)
        loss_send(level)
    loss_total = loss_wait(len(loss_peers) - 1)
    loss_ref[0, 0] = jnp.max(loss_total) / (4 * tok * nz)
    found = to_columns(exchange_wait(dots, dos_sem, dor_sem)) / width
    d3, d2, d1, d0, e32, e31, e30, e21, e20, e10 = (found[:, i : i + 1] for i in range(10))
    s3 = d3
    s2 = d2 - s3 * e32
    s1 = d1 - s3 * e31 - s2 * e21
    s0 = d0 - s3 * e30 - s2 * e20 - s1 * e10
    value = cotangent.astype(F32)

    def hand_out(slot_index):
        pltpu.make_async_copy(ys.at[core, slot_index], out.at[0, slot_index, core], loc_sem.at[slot_index]).start()
        begin(
            remote(
                ys.at[other, slot_index], out.at[0, slot_index, core], os_sem.at[slot_index], or_sem.at[slot_index], mate
            )
        )

    for c, stat in ((3, s3), (2, s2), (1, s1), (0, s0)):
        fresh = (lift(c, value) - saved(c) * (inv[c] ** 3 * stat)).astype(BF16)
        ys[SPAN_AT[c]] = fresh
        value = fresh.astype(F32)
        if c == 2:
            hand_out(1)
    hand_out(0)

    for slot_index in (1, 0):
        pltpu.make_async_copy(
            ys.at[core, slot_index], out.at[0, slot_index, core], loc_sem.at[slot_index]
        ).wait()
        slot = out.at[0, slot_index, other]
        remote(slot, slot, os_sem.at[slot_index], or_sem.at[slot_index], mate).wait_recv()
    for copies in ring_copies:
        for copy in copies[-2:]:
            copy.wait_send()
    for copy in sent:
        copy.wait_send()


def solution(mesh):
    n_seq, n_voc = mesh.shape["seq"], mesh.shape["vocab"]
    nz = n_seq // 2

    def per_device(hidden, head_weight, teacher_logits, targets, span_inputs, span_gains, span_weights):
        _, tok, width = hidden.shape
        rows, shard = head_weight.shape
        cols = shard // 2
        slice_width = span_inputs.shape[4]
        heads = span_weights.shape[2]
        plane = 2 * n_voc
        levels = 1 + (nz.bit_length() - 1)
        half = nz // 2
        dma = pltpu.SemaphoreType.DMA
        any_space = pl.BlockSpec(memory_space=pltpu.HBM)
        grads, loss = pl.pallas_call(
            functools.partial(kernel, nz, n_voc),
            out_shape=(
                jax.ShapeDtypeStruct((1, 2, 2, tok, slice_width), BF16),
                jax.ShapeDtypeStruct((1, 1), F32),
            ),
            in_specs=[any_space] * 7,
            out_specs=(any_space, pl.BlockSpec(memory_space=pltpu.SMEM)),
            scratch_shapes=[
                pltpu.VMEM((2, width, cols), BF16),
                pltpu.VMEM((2, tok, width), BF16),
                pltpu.VMEM((2, 2, tok, cols), BF16),
                pltpu.VMEM((2, 2, tok), jnp.int32),
                pltpu.VMEM((2, 2 * tok, cols), F32),
                pltpu.VMEM((2, 2 * tok, cols), F32),
                pltpu.VMEM((2, 2 * tok, cols), BF16),
                pltpu.VMEM((plane, 8, 2 * tok), F32),
                pltpu.VMEM((4, n_voc // 2, tok // 2, slice_width), BF16),
                pltpu.VMEM((4, n_voc // 2, tok // 2, slice_width), BF16),
                pltpu.VMEM((n_voc // 2, 4, tok // 2, slice_width), BF16),
                pltpu.VMEM((n_voc // 2, 4, tok // 2, slice_width), BF16),
                pltpu.VMEM((4, tok // 2, slice_width), BF16),
                pltpu.VMEM((4, tok // 2, slice_width), BF16),
                pltpu.VMEM((n_voc // 2, tok // 2, slice_width), BF16),
                pltpu.VMEM((n_voc // 2, tok // 2, slice_width), BF16),
                pltpu.VMEM((2, 2, tok, slice_width), BF16),
                pltpu.VMEM((2, 2, slice_width), F32),
                pltpu.VMEM((2, 2, heads, HEAD, HEAD), BF16),
                pltpu.VMEM((4, tok, slice_width), F32),
                pltpu.VMEM((n_voc, 8, tok), F32),
                pltpu.VMEM((n_voc, 16, tok), F32),
                pltpu.VMEM((levels, 8, 128), F32),
                pltpu.VMEM((levels, 8, 128), F32),
                pltpu.VMEM((2, 2, tok, slice_width), BF16),
                dma((7,)),
                dma((2, 4 * half - 2)),
                dma((2, 4 * half - 2)),
                dma((4 * nz,)),
                dma((4 * nz,)),
                dma((10,)),
                dma((10,)),
                dma((plane,)),
                dma((plane,)),
                dma((4, n_voc // 2)),
                dma((4, n_voc // 2)),
                dma((n_voc // 2, 4)),
                dma((n_voc // 2, 4)),
                dma((4,)),
                dma((4,)),
                dma((n_voc // 2,)),
                dma((n_voc // 2,)),
                dma((n_voc,)),
                dma((n_voc,)),
                dma((n_voc,)),
                dma((n_voc,)),
                dma((levels,)),
                dma((levels,)),
                dma((2,)),
                dma((2,)),
            ],
            compiler_params=pltpu.CompilerParams(
                collective_id=0, has_side_effects=True, vmem_limit_bytes=60 * 1024 * 1024
            ),
        )(hidden, head_weight, teacher_logits, targets, span_inputs, span_gains, span_weights)
        return grads, loss.reshape(())

    placed = (
        P(None, "seq", None),
        P("seq", ("section", "vocab")),
        P(None, "seq", ("section", "vocab")),
        P(None, "seq"),
        P("section", None, None, "seq", "vocab"),
        P("section", None, "vocab"),
        P("section", None, "vocab", None, None),
    )
    return jax.shard_map(
        per_device,
        mesh=mesh,
        in_specs=placed,
        out_specs=(P("section", None, None, "seq", "vocab"), P()),
        check_vma=False,
    )
```

profile of v0, /device:TPU:1, one launch (start us, length us, event | category | flops | bytes accessed | tf_op | source)
XLA Modules:
  0.0 106.8 jit_solution(13699289543478303977)
XLA Ops:
  0.6 102.6 %shard_map.86 = (bf16[1,2,2,128,512]{4,3,2,1,0:T(8,128)(2,1)}, f32[1,1]{1,0:T(1,128)}) custom-call(bf16[2,128,4096]{2,1,0:T(8,128)(2,1)} %hidden.1, bf16[256,1280]{1,0:T(8,128)(2,1)} %head.1, bf16[2,128,1280]{2,1,0:T(8,128)(2,1)} %teacher.1, s32[2,128]{1,0:T(2,128)} %targets.1, bf16[1,2,2,128,512]{4,3,2,1,0:T(8,128)(2,1)} %xin.1, f32[1,2,512]{2,1,0:T(2,128)} %gains.1, ...), custom_call_target="tpu_custom_call" | custom-call | tf_op jit(solution)/shard_map/pallas_call | solution.py:564
  103.2 1.9 %copy.11 = bf16[1,2,2,128,512]{4,3,2,1,0:T(8,128)(2,1)} copy(bf16[1,2,2,128,512]{4,3,2,1,0:T(8,128)(2,1)} %get-tuple-element.8) | data formatting | bytes 1048576
where the time goes:
time: 107 us
  Pallas kernels  103 us (96%)
  between operations  2.34 us (2%)
  local copies, waits for them, and re-layouts  1.87 us (2%)
    pallas_call x1, Pallas kernels, per_device(): pl.pallas_call(functools.partial(kernel, nz, n_voc), out_shape=(jax.Shape...  103 us

commit v1 on v0

--- a/solution.py
+++ b/solution.py
@@ -45,10 +45,10 @@
     nz, nv,
     hidden, head, teacher, targets, xin, gains, wspan,
     out, loss_ref,
-    wbuf, hid, tea, tgt, logits, texp, dlog, stats, snd_x, rcv_x, snd_y, rcv_y, two_x, end_x, two_y, end_y, xs, gs, ws, branch,
-    sq, dots, lsend, lrecv, ys,
+    wbuf, hid, tea, tgt, logits, texp, dlog, stats, snd_x, rcv_x, snd_y, rcv_y, two_x, end_x, two_y, end_y, xs, gs, ws,
+    sq, dots, vec_y, vec_x, told, heard, own_loss, losses, ys,
     loc_sem, zs_sem, zr_sem, ds_sem, dr_sem, ms_sem, mr_sem, sts_sem, str_sem, xs_sem, xr_sem, ys_sem, yr_sem,
-    exs_sem, exr_sem, eys_sem, eyr_sem,    sqs_sem, sqr_sem, dos_sem, dor_sem, ls_sem, lr_sem, os_sem, or_sem,
+    exs_sem, exr_sem, eys_sem, eyr_sem,    sqs_sem, sqr_sem, dos_sem, dor_sem, los_sem, lor_sem, vys_sem, vyr_sem, vxs_sem, vxr_sem, tos_sem, tor_sem, os_sem, or_sem,
 ):
     core = lax.axis_index("section")
     seq = lax.axis_index("seq")
@@ -62,12 +62,18 @@
     slice_width = xs.shape[3]
     plane = 2 * nv
     me = xh * nv + voc
+    half_tok = tok // 2
+    ny = nv // 2
+    xi, yi = xh * 2 + xl, voc // 2
 
     def at(c, zz, hh, v):
         return (c, zz * 2 + hh, v)
 
     def plane_peer(index):
         return at(core, z, index // nv, index % nv)
+
+    def in_plane(x, y):
+        return at(core, z, x // 2, y * 2 + x % 2)
 
     mate = at(other, z, xh, voc)
     partner = at(core, z, 1 - xh, voc)
@@ -75,14 +81,8 @@
     near = at(core, z, 1 - xh, voc + 1 - 2 * xl)
     right = at(core, (z + 1) % nz, xh, voc)
     left = at(core, (z + nz - 1) % nz, xh, voc)
-    far = []
-    bit = 1
-    while bit < nz:
-        far.append(at(core, z + bit - 2 * bit * ((z // bit) % 2), xh, voc))
-        bit *= 2
-
     barrier = pltpu.get_barrier_semaphore()
-    direct = [mate, partner_mate, right, left] + far[1:]
+    direct = [mate, partner_mate, right, left]
     for peer in direct:
         pl.semaphore_signal(barrier, inc=1, device_id=peer, device_id_type=MESH)
 
@@ -249,10 +249,6 @@
         squares.append(jnp.sum(value * value, axis=1, keepdims=True))
     sq[voc] = to_rows(squares, 8)
     exchange(sq, sqs_sem, sqr_sem)
-    for c in range(4):
-        scaled = (saved(c) * gain(c)).astype(BF16)
-        branch[c] = heads_dot(scaled, ws[SPAN_AT[c]], False)
-
     def multiply(delta, first=False):
         for part in range(4):
             mate_wait(delta, part)
@@ -271,27 +267,41 @@
         remote(slot, slot, ms_sem.at[5], mr_sem.at[5], near).wait_recv()
 
     def span_ready():
-        total = to_columns(exchange_wait(sq, sqs_sem, sqr_sem))
-        inv = [lax.rsqrt(total[:, c : c + 1] / width + EPS) for c in range(4)]
-
-        def lift(c, value):
-            grad = heads_dot(value.astype(BF16), ws[SPAN_AT[c]], True)
-            return value + inv[c] * gain(c) * grad
+        inv_rows = lax.rsqrt(exchange_wait(sq, sqs_sem, sqr_sem) / width + EPS)
+        total = to_columns(inv_rows)
+        inv = [total[:, c : c + 1] for c in range(4)]
+
+        def back(c, value):
+            return value + inv[c] * heads_dot((value * gain(c)).astype(BF16), ws[SPAN_AT[c]], False)
 
         def inner(c, value):
-            return jnp.sum(value * branch[c], axis=1, keepdims=True)
-
-        u3 = saved(3) * inv[3] ** 3
-        e32 = inner(2, u3)
-        v = lift(2, u3)
-        e31 = inner(1, v)
-        v = lift(1, v)
-        e30 = inner(0, v)
-        u2 = saved(2) * inv[2] ** 3
-        e21 = inner(1, u2)
-        e20 = inner(0, lift(1, u2))
-        e10 = inner(0, saved(1) * inv[1] ** 3)
-        return inv, lift, inner, [e32, e31, e30, e21, e20, e10]
+            return jnp.sum(saved(c) * inv[c] ** 3 * value, axis=1, keepdims=True)
+
+        products = []
+        for c in range(4):
+            value = heads_dot((saved(c) * gain(c)).astype(BF16), ws[SPAN_AT[c]], False)
+            for upper in range(c + 1, 4):
+                products.append(inner(upper, value))
+                value = back(upper, value)
+            vec_y[yi, c] = value[:half_tok].astype(BF16)
+            vec_x[xi, c] = value[half_tok:].astype(BF16)
+        dots[voc] = to_rows(products, 8)
+        exchange(dots, dos_sem, dor_sem)
+        return inv, inv_rows
+
+    def vectors_send():
+        for oy in range(1, ny):
+            begin(remote(vec_y.at[yi], vec_y.at[yi], vys_sem.at[oy], vyr_sem.at[oy], in_plane(xi, (yi + oy) % ny)))
+        for ox in range(1, 4):
+            begin(remote(vec_x.at[xi], vec_x.at[xi], vxs_sem.at[ox], vxr_sem.at[ox], in_plane((xi + ox) % 4, yi)))
+
+    def vectors_wait():
+        for oy in range(1, ny):
+            slot = vec_y.at[(yi + ny - oy) % ny]
+            remote(slot, slot, vys_sem.at[oy], vyr_sem.at[oy], mate).wait_recv()
+        for ox in range(1, 4):
+            slot = vec_x.at[(xi + 4 - ox) % 4]
+            remote(slot, slot, vxs_sem.at[ox], vxr_sem.at[ox], mate).wait_recv()
 
     def teacher_ready():
         pairs = ((other, xh, 4, mate), (core, 1 - xh, 7, partner), (other, 1 - xh, 8, partner_mate))
@@ -316,9 +326,10 @@
         for way in (0, 1):
             ring_send(way, i)
         if i == 5:
-            inv, lift, inner, cross_spans = span_ready()
+            inv, inv_rows = span_ready()
     teacher_top, teacher_total = teacher_ready()
     hidden_wait()
+    vectors_send()
     multiply(0, first=True)
     for i in range(ring_count - 4, ring_count):
         for way in (0, 1):
@@ -328,6 +339,8 @@
                 multiply(-d)
                 multiply(d)
     multiply(half)
+    cross_rows = exchange_wait(dots, dos_sem, dor_sem)
+    vectors_wait()
 
     def target_column():
         parts = []
@@ -387,31 +400,34 @@
     student_scale = jnp.exp(student_top - scales[:, 0:1])
     teacher_scale = jnp.exp(teacher_top - scales[:, 1:2])
 
-    loss_peers = [mate] + far
-    lsend[0] = jnp.broadcast_to(jnp.sum(terms, axis=1, keepdims=True), (8, 128))
-
-    def loss_send(level):
-        begin(remote(lsend.at[level], lrecv.at[level], ls_sem.at[level], lr_sem.at[level], loss_peers[level]))
-
-    def loss_wait(level):
-        slot = lrecv.at[level]
-        remote(slot, slot, ls_sem.at[level], lr_sem.at[level], mate).wait_recv()
-        return lsend[level] + lrecv[level]
-
-    loss_send(0)
+    own_loss[0] = jnp.broadcast_to(jnp.sum(terms, axis=1, keepdims=True), (8, 128))
+    begin(remote(own_loss.at[0], own_loss.at[1], los_sem.at[0, 0], lor_sem.at[0, 0], mate))
+
+    def loss_start():
+        remote(own_loss.at[1], own_loss.at[1], los_sem.at[0, 0], lor_sem.at[0, 0], mate).wait_recv()
+        losses[z] = own_loss[0] + own_loss[1]
+        loss_send(1)
+
+    def loss_send(k):
+        for way, peer in ((0, right), (1, left)):
+            if k < half or way == 0:
+                slot = losses.at[(z + nz - (k - 1)) % nz if way == 0 else (z + k - 1) % nz]
+                begin(remote(slot, slot, los_sem.at[way, k], lor_sem.at[way, k], peer))
+
+    def loss_wait(k):
+        for way in (0, 1):
+            if k < half or way == 0:
+                slot = losses.at[(z + nz - k) % nz if way == 0 else (z + k) % nz]
+                remote(slot, slot, los_sem.at[way, k], lor_sem.at[way, k], right).wait_recv()
+        if k < half:
+            loss_send(k + 1)
 
     for s in (0, 1):
         value = (1.0 + CE_WEIGHT) * (logits[s] * student_scale) - texp[s] * teacher_scale
         value = value - jnp.where(hit(s), CE_WEIGHT, 0.0)
         dlog[s] = (LOSS_SCALE * value).astype(BF16)
 
-    half_tok = tok // 2
-    ny = nv // 2
-    xi, yi = xh * 2 + xl, voc // 2
     nt = (((1,), (1,)), ((), ()))
-
-    def in_plane(x, y):
-        return at(core, z, x // 2, y * 2 + x % 2)
 
     def slice_turn(i, carry):
         oy = (i // 2 + 1) % ny
@@ -443,9 +459,7 @@
         return carry
 
     lax.fori_loop(0, nv, slice_turn, 0)
-    if len(loss_peers) > 1:
-        lsend[1] = loss_wait(0)
-        loss_send(1)
+    loss_start()
 
     def sum_x(oy):
         y = (yi + oy) % ny
@@ -465,13 +479,90 @@
             total = total + slot[...].astype(F32)
         return total
 
+    def fold(value):
+        parts = [value[:, i : i + 128] for i in range(0, slice_width, 128)]
+        return functools.reduce(lambda a, b: a + b, parts)
+
+    def products_with(vectors, value):
+        return [fold(vectors[c].astype(F32) * value) for c in range(4)]
+
+    def add(left_list, right_list):
+        return [a + b for a, b in zip(left_list, right_list)]
+
+    first_products = [jnp.zeros((half_tok, 128), F32)] * 4
     for oy in range(1, ny):
-        two_y[oy] = sum_x(oy).astype(BF16)
+        value = sum_x(oy)
+        two_y[oy] = value.astype(BF16)
         begin(remote(two_y.at[oy], end_y.at[oy], eys_sem.at[oy], eyr_sem.at[oy], in_plane(xi, (yi + oy) % ny)))
+        first_products = add(first_products, products_with(vec_y[(yi + oy) % ny], value))
+    loss_wait(1)
+    first_half = sum_x(0)
+    first_products = add(first_products, products_with(vec_y[yi], first_half))
+    column_sums = {}
     for ox in range(1, 4):
-        two_x[ox] = sum_y(ox).astype(BF16)
+        column_sums[ox] = sum_y(ox)
+        two_x[ox] = column_sums[ox].astype(BF16)
         begin(remote(two_x.at[ox], end_x.at[ox], exs_sem.at[ox], exr_sem.at[ox], in_plane((xi + ox) % 4, yi)))
-    first_half, second_half = sum_x(0), sum_y(0)
+    second_half = sum_y(0)
+    column_sums[0] = second_half
+    near_products = [jnp.zeros((half_tok, 128), F32)] * 4
+    away_products = near_products
+    for ox in range(4):
+        x = (xi + ox) % 4
+        found = products_with(vec_x[x], column_sums[ox])
+        same = x // 2 == xh
+        near_products = [a + jnp.where(same, b, 0.0) for a, b in zip(near_products, found)]
+        away_products = [a + jnp.where(same, 0.0, b) for a, b in zip(away_products, found)]
+
+    def message(first_part, second_part):
+        columns = [
+            jnp.sum(jnp.concatenate([a, b], axis=0), axis=1, keepdims=True) for a, b in zip(first_part, second_part)
+        ]
+        return to_rows(columns, 8)
+
+    away = message([jnp.zeros((half_tok, 128), F32)] * 4, away_products)
+    close = message(first_products, near_products)
+    told[0] = jnp.where(xh == 0, close, away)
+    told[1] = jnp.where(xh == 0, away, close)
+
+    def told_send(i, carry):
+        to = (me + i) % plane
+        remote(told.at[to // nv], heard.at[me], tos_sem.at[i], tor_sem.at[i], plane_peer(to)).start()
+        return carry
+
+    def told_wait(i, carry):
+        src = (me + plane - i) % plane
+        remote(heard.at[src], heard.at[src], tos_sem.at[i], tor_sem.at[i], mate).wait_recv()
+        remote(told.at[0], heard.at[me], tos_sem.at[i], tor_sem.at[i], mate).wait_send()
+        return carry
+
+    lax.fori_loop(1, plane, told_send, 0)
+    heard[me] = close
+
+    def slice_sent(i, carry):
+        oy, ox = i // 4, i % 4
+
+        @pl.when(ox != 0)
+        def _():
+            x, y = (xi + ox) % 4, (yi + oy) % ny
+            remote(snd_x.at[x, y], rcv_x.at[xi, y], xs_sem.at[ox, oy], xr_sem.at[ox, oy], mate).wait_send()
+
+        @pl.when(oy != 0)
+        def _():
+            x, y = (xi + ox) % 4, (yi + oy) % ny
+            remote(snd_y.at[y, x], rcv_y.at[yi, x], ys_sem.at[oy, ox], yr_sem.at[oy, ox], mate).wait_send()
+
+        return carry
+
+    lax.fori_loop(0, 4 * ny, slice_sent, 0)
+
+    loss_wait(2)
+    for copies in ring_copies:
+        for copy in copies[-2:]:
+            copy.wait_send()
+    for copy in sent:
+        copy.wait_send()
+    sent.clear()
     for oy in range(1, ny):
         remote(end_y.at[oy], end_y.at[oy], eys_sem.at[oy], eyr_sem.at[oy], mate).wait_recv()
         first_half = first_half + end_y[oy].astype(F32)
@@ -480,42 +571,18 @@
         second_half = second_half + end_x[ox].astype(F32)
     cotangent = jnp.concatenate([first_half.astype(BF16), second_half.astype(BF16)], axis=0)
 
-    def slice_sent(i, carry):
-        oy, ox = i // 4, i % 4
-
-        @pl.when(ox != 0)
-        def _():
-            x, y = (xi + ox) % 4, (yi + oy) % ny
-            remote(snd_x.at[x, y], rcv_x.at[xi, y], xs_sem.at[ox, oy], xr_sem.at[ox, oy], mate).wait_send()
-
-        @pl.when(oy != 0)
-        def _():
-            x, y = (xi + ox) % 4, (yi + oy) % ny
-            remote(snd_y.at[y, x], rcv_y.at[yi, x], ys_sem.at[oy, ox], yr_sem.at[oy, ox], mate).wait_send()
-
-        return carry
-
-    lax.fori_loop(0, 4 * ny, slice_sent, 0)
-
-    value = cotangent.astype(F32)
-    products = [inner(3, value)]
-    for c in (3, 2, 1):
-        value = lift(c, value)
-        products.append(inner(c - 1, value))
-    dots[voc] = to_rows(products + cross_spans, 16)
-    exchange(dots, dos_sem, dor_sem)
-    for level in range(2, len(loss_peers)):
-        lsend[level] = loss_wait(level - 1)
-        loss_send(level)
-    loss_total = loss_wait(len(loss_peers) - 1)
-    loss_ref[0, 0] = jnp.max(loss_total) / (4 * tok * nz)
-    found = to_columns(exchange_wait(dots, dos_sem, dor_sem)) / width
-    d3, d2, d1, d0, e32, e31, e30, e21, e20, e10 = (found[:, i : i + 1] for i in range(10))
+    lax.fori_loop(1, plane, told_wait, 0)
+    found = heard[0]
+    for i in range(1, plane):
+        found = found + heard[i]
+    d0, d1, d2, d3 = (found[c : c + 1] / width for c in range(4))
+    e10, e20, e30, e21, e31, e32 = (cross_rows[c : c + 1] / width for c in range(6))
     s3 = d3
     s2 = d2 - s3 * e32
     s1 = d1 - s3 * e31 - s2 * e21
     s0 = d0 - s3 * e30 - s2 * e20 - s1 * e10
-    value = cotangent.astype(F32)
+    pull = to_columns(inv_rows[0:4] ** 3 * jnp.concatenate([s0, s1, s2, s3], axis=0))
+    value = cotangent
 
     def hand_out(slot_index):
         pltpu.make_async_copy(ys.at[core, slot_index], out.at[0, slot_index, core], loc_sem.at[slot_index]).start()
@@ -525,23 +592,26 @@
             )
         )
 
-    for c, stat in ((3, s3), (2, s2), (1, s1), (0, s0)):
-        fresh = (lift(c, value) - saved(c) * (inv[c] ** 3 * stat)).astype(BF16)
-        ys[SPAN_AT[c]] = fresh
-        value = fresh.astype(F32)
+    for c in (3, 2, 1, 0):
+        grad = heads_dot(value, ws[SPAN_AT[c]], True)
+        fresh = value.astype(F32) + inv[c] * gain(c) * grad - saved(c) * pull[:, c : c + 1]
+        value = fresh.astype(BF16)
+        ys[SPAN_AT[c]] = value
         if c == 2:
             hand_out(1)
     hand_out(0)
-
+    for k in range(3, half + 1):
+        loss_wait(k)
+    loss_total = losses[0]
+    for i in range(1, nz):
+        loss_total = loss_total + losses[i]
+    loss_ref[0, 0] = jnp.max(loss_total) / (4 * tok * nz)
     for slot_index in (1, 0):
         pltpu.make_async_copy(
             ys.at[core, slot_index], out.at[0, slot_index, core], loc_sem.at[slot_index]
         ).wait()
         slot = out.at[0, slot_index, other]
         remote(slot, slot, os_sem.at[slot_index], or_sem.at[slot_index], mate).wait_recv()
-    for copies in ring_copies:
-        for copy in copies[-2:]:
-            copy.wait_send()
     for copy in sent:
         copy.wait_send()
 
@@ -557,10 +627,13 @@
         slice_width = span_inputs.shape[4]
         heads = span_weights.shape[2]
         plane = 2 * n_voc
-        levels = 1 + (nz.bit_length() - 1)
         half = nz // 2
         dma = pltpu.SemaphoreType.DMA
-        any_space = pl.BlockSpec(memory_space=pltpu.HBM)
+        any_space = pl.BlockSpec(memory_space=pl.ANY)
+        operands = [
+            pltpu.with_memory_space_constraint(a, pltpu.HBM)
+            for a in (hidden, head_weight, teacher_logits, targets, span_inputs, span_gains, span_weights)
+        ]
         grads, loss = pl.pallas_call(
             functools.partial(kernel, nz, n_voc),
             out_shape=(
@@ -589,11 +662,14 @@
                 pltpu.VMEM((2, 2, tok, slice_width), BF16),
                 pltpu.VMEM((2, 2, slice_width), F32),
                 pltpu.VMEM((2, 2, heads, HEAD, HEAD), BF16),
-                pltpu.VMEM((4, tok, slice_width), F32),
                 pltpu.VMEM((n_voc, 8, tok), F32),
-                pltpu.VMEM((n_voc, 16, tok), F32),
-                pltpu.VMEM((levels, 8, 128), F32),
-                pltpu.VMEM((levels, 8, 128), F32),
+                pltpu.VMEM((n_voc, 8, tok), F32),
+                pltpu.VMEM((n_voc // 2, 4, tok // 2, slice_width), BF16),
+                pltpu.VMEM((4, 4, tok // 2, slice_width), BF16),
+                pltpu.VMEM((2, 8, tok), F32),
+                pltpu.VMEM((plane, 8, tok), F32),
+                pltpu.VMEM((2, 8, 128), F32),
+                pltpu.VMEM((nz, 8, 128), F32),
                 pltpu.VMEM((2, 2, tok, slice_width), BF16),
                 dma((7,)),
                 dma((2, 4 * half - 2)),
@@ -616,15 +692,21 @@
                 dma((n_voc,)),
                 dma((n_voc,)),
                 dma((n_voc,)),
-                dma((levels,)),
-                dma((levels,)),
+                dma((2, half + 1)),
+                dma((2, half + 1)),
+                dma((n_voc // 2,)),
+                dma((n_voc // 2,)),
+                dma((4,)),
+                dma((4,)),
+                dma((plane,)),
+                dma((plane,)),
                 dma((2,)),
                 dma((2,)),
             ],
             compiler_params=pltpu.CompilerParams(
-                collective_id=0, has_side_effects=True, vmem_limit_bytes=60 * 1024 * 1024
+                collective_id=0, has_side_effects=True, vmem_limit_bytes=48 * 1024 * 1024
             ),
-        )(hidden, head_weight, teacher_logits, targets, span_inputs, span_gains, span_weights)
+        )(*operands)
         return grads, loss.reshape(())
 
     placed = (

time: 107 us -> 104 us (0.972)
  Pallas kernels: 103 us -> 101 us
  local copies, waits for them, and re-layouts: 1.87 us -> 0.8 us
    pallas_call x1, Pallas kernels: 103 us -> 101 us  [per_device(): pl.pallas_call(functools.partial(kernel, nz, n_voc), out_shape=(jax.Shape...]
    unnamed x1, local copies, waits for them, and re-layouts: 1.87 us -> 0.8 us
where the time goes in v1:
time: 104 us
  Pallas kernels  101 us (97%)
  between operations  2.33 us (2%)
    pallas_call x1, Pallas kernels, per_device(): pl.pallas_call(functools.partial(kernel, nz, n_voc), out_shape=(jax.Shape...  101 us

profile of v1, /device:TPU:1, one launch (start us, length us, event | category | flops | bytes accessed | tf_op | source)
XLA Modules:
  0.0 103.8 jit_solution(3820970008349023535)
XLA Ops:
  0.6 100.7 %shard_map.86 = (bf16[1,2,2,128,512]{4,3,2,1,0:T(8,128)(2,1)S(1)}, f32[1,1]{1,0:T(1,128)}) custom-call(bf16[2,128,4096]{2,1,0:T(8,128)(2,1)} %hidden.1, bf16[256,1280]{1,0:T(8,128)(2,1)} %head.1, bf16[2,128,1280]{2,1,0:T(8,128)(2,1)} %teacher.1, s32[2,128]{1,0:T(2,128)} %targets.1, bf16[1,2,2,128,512]{4,3,2,1,0:T(8,128)(2,1)} %xin.1, f32[1,2,512]{2,1,0:T(2,128)} %gains.1, ...), custom_call_target="tpu_custom_call" | custom-call | tf_op jit(solution)/shard_map/pallas_call | solution.py:637
  101.3 0.8 copy.11

commit v2 on v1

--- a/solution.py
+++ b/solution.py
@@ -45,7 +45,7 @@
     nz, nv,
     hidden, head, teacher, targets, xin, gains, wspan,
     out, loss_ref,
-    wbuf, hid, tea, tgt, logits, texp, dlog, stats, snd_x, rcv_x, snd_y, rcv_y, two_x, end_x, two_y, end_y, xs, gs, ws,
+    wbuf, hid, tea, tgt, logits, texp, dlog, stats, snd_x, rcv_x, pass_x, snd_y, rcv_y, pass_y, two_x, end_x, two_y, end_y, xs, gs, ws,
     sq, dots, vec_y, vec_x, told, heard, own_loss, losses, ys,
     loc_sem, zs_sem, zr_sem, ds_sem, dr_sem, ms_sem, mr_sem, sts_sem, str_sem, xs_sem, xr_sem, ys_sem, yr_sem,
     exs_sem, exr_sem, eys_sem, eyr_sem,    sqs_sem, sqr_sem, dos_sem, dor_sem, los_sem, lor_sem, vys_sem, vyr_sem, vxs_sem, vxr_sem, tos_sem, tor_sem, os_sem, or_sem,
@@ -289,9 +289,11 @@
         exchange(dots, dos_sem, dor_sem)
         return inv, inv_rows
 
-    def vectors_send():
+    def vectors_y_send():
         for oy in range(1, ny):
             begin(remote(vec_y.at[yi], vec_y.at[yi], vys_sem.at[oy], vyr_sem.at[oy], in_plane(xi, (yi + oy) % ny)))
+
+    def vectors_x_send():
         for ox in range(1, 4):
             begin(remote(vec_x.at[xi], vec_x.at[xi], vxs_sem.at[ox], vxr_sem.at[ox], in_plane((xi + ox) % 4, yi)))
 
@@ -327,20 +329,26 @@
             ring_send(way, i)
         if i == 5:
             inv, inv_rows = span_ready()
-    teacher_top, teacher_total = teacher_ready()
-    hidden_wait()
-    vectors_send()
-    multiply(0, first=True)
+            vectors_y_send()
+        if i == ring_count - 2:
+            teacher_top, teacher_total = teacher_ready()
+            hidden_wait()
+            vectors_x_send()
+            multiply(0, first=True)
+            for d in range(1, half - 2):
+                multiply(-d)
+                multiply(d)
     for i in range(ring_count - 4, ring_count):
         for way in (0, 1):
             ring_wait(way, i)
-        if i == ring_count - 3:
-            for d in range(1, half):
+        if i == ring_count - 4:
+            for d in range(max(1, half - 2), half - 1):
                 multiply(-d)
                 multiply(d)
+        if i == ring_count - 3:
+            multiply(1 - half)
+            multiply(half - 1)
     multiply(half)
-    cross_rows = exchange_wait(dots, dos_sem, dor_sem)
-    vectors_wait()
 
     def target_column():
         parts = []
@@ -427,12 +435,37 @@
         value = value - jnp.where(hit(s), CE_WEIGHT, 0.0)
         dlog[s] = (LOSS_SCALE * value).astype(BF16)
 
+    quarter = tok // 4
+    upper, lower = pl.ds(0, quarter), pl.ds(quarter, quarter)
     nt = (((1,), (1,)), ((), ()))
 
+    def x_peer(step):
+        return in_plane((xi + step + 4) % 4, yi)
+
+    def y_peer(step):
+        return in_plane(xi, (yi + step + ny) % ny)
+
+    def stage_x(kind, way, y):
+        step = 1 - 2 * way
+        part = (upper, lower)[way if kind != 1 else 1 - way]
+        source = snd_x.at[(xi + 2) % 4 if kind == 0 else (xi + step + 4) % 4, y, part]
+        target = pass_x.at[way, y] if kind == 0 else rcv_x.at[way, y, part]
+        return remote(source, target, xs_sem.at[kind, way, y], xr_sem.at[kind, way, y], x_peer(step))
+
+    def stage_y(kind, way, x):
+        step = 1 - 2 * way
+        part = (upper, lower)[way if kind != 1 else 1 - way]
+        source = snd_y.at[(yi + 2) % ny if kind == 0 else (yi + step + ny) % ny, x, part]
+        target = pass_y.at[way, x] if kind == 0 else rcv_y.at[way, x, part]
+        return remote(source, target, ys_sem.at[kind, way, x], yr_sem.at[kind, way, x], y_peer(step))
+
+    def offset(i):
+        return jnp.where(i == 0, 2, jnp.where(i == 1, 1, jnp.where(i == 2, 3, 0)))
+
     def slice_turn(i, carry):
-        oy = (i // 2 + 1) % ny
+        oy = offset(i // 2)
         y = (yi + oy) % ny
-        lo = (xl + 1 + i) % 2
+        lo = (xl + i) % 2
         v = y * 2 + lo
         span = pl.ds(pl.multiple_of(v * slice_width, slice_width), slice_width)
         part = lax.dot_general(dlog[0], wbuf[0, span, :], nt, preferred_element_type=F32)
@@ -440,43 +473,76 @@
         part = part.astype(BF16)
         for hh in (0, 1):
             x = hh * 2 + lo
-            ox = (x - xi + 4) % 4
             snd_x[x, y] = part[hh * tok : hh * tok + half_tok]
             snd_y[y, x] = part[hh * tok + half_tok : (hh + 1) * tok]
 
-            @pl.when(ox != 0)
+        @pl.when(i % 2 == 0)
+        def _():
+            for way in (0, 1):
+                stage_x(0, way, y).start()
+
+        @pl.when(i % 2 == 1)
+        def _():
+            for way in (0, 1):
+                stage_x(1, way, y).start()
+
+        for hh in (0, 1):
+
+            @pl.when(oy == 2)
             def _():
-                remote(
-                    snd_x.at[x, y], rcv_x.at[xi, y], xs_sem.at[ox, oy], xr_sem.at[ox, oy], in_plane(x, yi)
-                ).start()
-
-            @pl.when(oy != 0)
+                for way in (0, 1):
+                    stage_y(0, way, hh * 2 + lo).start()
+
+            @pl.when(oy == 1)
             def _():
-                remote(
-                    snd_y.at[y, x], rcv_y.at[yi, x], ys_sem.at[oy, ox], yr_sem.at[oy, ox], in_plane(xi, y)
-                ).start()
+                stage_y(1, 0, hh * 2 + lo).start()
+
+            @pl.when(oy == 3)
+            def _():
+                stage_y(1, 1, hh * 2 + lo).start()
 
         return carry
 
     lax.fori_loop(0, nv, slice_turn, 0)
+
+    def pass_turn(i, carry):
+        y = (yi + offset(i)) % ny
+        for way in (0, 1):
+            step = 1 - 2 * way
+            part = (upper, lower)[way]
+            stage_x(0, way, y).wait_recv()
+            x = (xi + step + 4) % 4
+            total = snd_x[x, y, part].astype(F32) + pass_x[way, y].astype(F32)
+            snd_x[x, y, part] = total.astype(BF16)
+            stage_x(2, way, y).start()
+            stage_y(0, way, i).wait_recv()
+            to = (yi + step + ny) % ny
+            total = snd_y[to, i, part].astype(F32) + pass_y[way, i].astype(F32)
+            snd_y[to, i, part] = total.astype(BF16)
+            stage_y(2, way, i).start()
+        return carry
+
+    lax.fori_loop(0, ny, pass_turn, 0)
     loss_start()
+    vectors_wait()
+    cross_rows = exchange_wait(dots, dos_sem, dor_sem)
 
     def sum_x(oy):
         y = (yi + oy) % ny
         total = snd_x[xi, y].astype(F32)
-        for ox in range(1, 4):
-            slot = rcv_x.at[(xi + 4 - ox) % 4, y]
-            remote(slot, slot, xs_sem.at[ox, oy], xr_sem.at[ox, oy], mate).wait_recv()
-            total = total + slot[...].astype(F32)
+        for way in (0, 1):
+            for kind in (1, 2):
+                stage_x(kind, way, y).wait_recv()
+            total = total + rcv_x[way, y].astype(F32)
         return total
 
     def sum_y(ox):
         x = (xi + ox) % 4
         total = snd_y[yi, x].astype(F32)
-        for oy in range(1, ny):
-            slot = rcv_y.at[(yi + ny - oy) % ny, x]
-            remote(slot, slot, ys_sem.at[oy, ox], yr_sem.at[oy, ox], mate).wait_recv()
-            total = total + slot[...].astype(F32)
+        for way in (0, 1):
+            for kind in (1, 2):
+                stage_y(kind, way, x).wait_recv()
+            total = total + rcv_y[way, x].astype(F32)
         return total
 
     def fold(value):
@@ -490,7 +556,7 @@
         return [a + b for a, b in zip(left_list, right_list)]
 
     first_products = [jnp.zeros((half_tok, 128), F32)] * 4
-    for oy in range(1, ny):
+    for oy in (2, 1, 3):
         value = sum_x(oy)
         two_y[oy] = value.astype(BF16)
         begin(remote(two_y.at[oy], end_y.at[oy], eys_sem.at[oy], eyr_sem.at[oy], in_plane(xi, (yi + oy) % ny)))
@@ -540,21 +606,13 @@
     heard[me] = close
 
     def slice_sent(i, carry):
-        oy, ox = i // 4, i % 4
-
-        @pl.when(ox != 0)
-        def _():
-            x, y = (xi + ox) % 4, (yi + oy) % ny
-            remote(snd_x.at[x, y], rcv_x.at[xi, y], xs_sem.at[ox, oy], xr_sem.at[ox, oy], mate).wait_send()
-
-        @pl.when(oy != 0)
-        def _():
-            x, y = (xi + ox) % 4, (yi + oy) % ny
-            remote(snd_y.at[y, x], rcv_y.at[yi, x], ys_sem.at[oy, ox], yr_sem.at[oy, ox], mate).wait_send()
-
+        for kind in range(3):
+            for way in (0, 1):
+                stage_x(kind, way, i).wait_send()
+                stage_y(kind, way, i).wait_send()
         return carry
 
-    lax.fori_loop(0, 4 * ny, slice_sent, 0)
+    lax.fori_loop(0, ny, slice_sent, 0)
 
     loss_wait(2)
     for copies in ring_copies:
@@ -652,9 +710,11 @@
                 pltpu.VMEM((2, 2 * tok, cols), BF16),
                 pltpu.VMEM((plane, 8, 2 * tok), F32),
                 pltpu.VMEM((4, n_voc // 2, tok // 2, slice_width), BF16),
-                pltpu.VMEM((4, n_voc // 2, tok // 2, slice_width), BF16),
+                pltpu.VMEM((2, n_voc // 2, tok // 2, slice_width), BF16),
+                pltpu.VMEM((2, n_voc // 2, tok // 4, slice_width), BF16),
                 pltpu.VMEM((n_voc // 2, 4, tok // 2, slice_width), BF16),
-                pltpu.VMEM((n_voc // 2, 4, tok // 2, slice_width), BF16),
+                pltpu.VMEM((2, 4, tok // 2, slice_width), BF16),
+                pltpu.VMEM((2, 4, tok // 4, slice_width), BF16),
                 pltpu.VMEM((4, tok // 2, slice_width), BF16),
                 pltpu.VMEM((4, tok // 2, slice_width), BF16),
                 pltpu.VMEM((n_voc // 2, tok // 2, slice_width), BF16),
@@ -680,10 +740,10 @@
                 dma((10,)),
                 dma((plane,)),
                 dma((plane,)),
-                dma((4, n_voc // 2)),
-                dma((4, n_voc // 2)),
-                dma((n_voc // 2, 4)),
-                dma((n_voc // 2, 4)),
+                dma((3, 2, n_voc // 2)),
+                dma((3, 2, n_voc // 2)),
+                dma((3, 2, 4)),
+                dma((3, 2, 4)),
                 dma((4,)),
                 dma((4,)),
                 dma((n_voc // 2,)),

time: 104 us -> 98.5 us (0.947)
  Pallas kernels: 101 us -> 95.3 us
    pallas_call x1, Pallas kernels: 101 us -> 95.3 us  [per_device(): pl.pallas_call(functools.partial(kernel, nz, n_voc), out_shape=(jax.Shape...]
where the time goes in v2:
time: 98.5 us
  Pallas kernels  95.3 us (97%)
  between operations  2.33 us (2%)
    pallas_call x1, Pallas kernels, per_device(): pl.pallas_call(functools.partial(kernel, nz, n_voc), out_shape=(jax.Shape...  95.3 us

profile of v2, /device:TPU:1, one launch (start us, length us, event | category | flops | bytes accessed | tf_op | source)
XLA Modules:
  0.0 98.5 jit_solution(3895902146323104138)
XLA Ops:
  0.6 95.3 %shard_map.86 = (bf16[1,2,2,128,512]{4,3,2,1,0:T(8,128)(2,1)S(1)}, f32[1,1]{1,0:T(1,128)}) custom-call(bf16[2,128,4096]{2,1,0:T(8,128)(2,1)} %hidden.1, bf16[256,1280]{1,0:T(8,128)(2,1)} %head.1, bf16[2,128,1280]{2,1,0:T(8,128)(2,1)} %teacher.1, s32[2,128]{1,0:T(2,128)} %targets.1, bf16[1,2,2,128,512]{4,3,2,1,0:T(8,128)(2,1)} %xin.1, f32[1,2,512]{2,1,0:T(2,128)} %gains.1, ...), custom_call_target="tpu_custom_call" | custom-call | tf_op jit(solution)/shard_map/pallas_call | solution.py:695
  96.0 0.8 copy.11

commit v3 on v2

--- a/solution.py
+++ b/solution.py
@@ -131,25 +131,30 @@
         k, part = ring_parts[way][i]
         slot = part_at(core, -(k - 1) if way == 0 else k - 1, part)
         src = own_part(part, xh) if k == 1 and part < 2 else slot
+        held = []
         if k > 1:
-            ring_wait(way, ring_parts[way].index((k - 1, part)))
+            held = ring_wait(way, ring_parts[way].index((k - 1, part)))
         if i >= 2:
             ring_copies[way][i - 2].wait_send()
         copy = remote(src, slot, zs_sem.at[way, i], zr_sem.at[way, i], right if way == 0 else left)
         copy.start()
         ring_copies[way].append(copy)
+        for come in held:
+            mate_send(*come)
 
     arrived = [0, 0]
 
     def ring_wait(way, i):
+        come = []
         while arrived[way] <= i:
             j = arrived[way]
             k, part = ring_parts[way][j]
             delta = -k if way == 0 else k
             slot = part_at(core, delta, part)
             remote(slot, slot, zs_sem.at[way, j], zr_sem.at[way, j], right).wait_recv()
-            mate_send(delta, part)
+            come.append((delta, part))
             arrived[way] += 1
+        return come
 
     def mate_send(delta, part):
         slot = part_at(core, delta, part)
@@ -250,12 +255,13 @@
     sq[voc] = to_rows(squares, 8)
     exchange(sq, sqs_sem, sqr_sem)
     def multiply(delta, first=False):
-        for part in range(4):
-            mate_wait(delta, part)
         zz = lax.rem(z + delta + nz, nz)
         span = pl.ds(pl.multiple_of(zz * 2 * rows, 2 * rows), 2 * rows)
         left_part = hid[:, :, span].reshape(2 * tok, 2 * rows)
-        for s in (0, 1):
+        for s in (core, other):
+            if s is other:
+                for part in range(4):
+                    mate_wait(delta, part)
             product = jnp.dot(left_part, wbuf[s, span, :], preferred_element_type=F32)
             if first:
                 logits[s] = product
@@ -340,7 +346,8 @@
                 multiply(d)
     for i in range(ring_count - 4, ring_count):
         for way in (0, 1):
-            ring_wait(way, i)
+            for come in ring_wait(way, i):
+                mate_send(*come)
         if i == ring_count - 4:
             for d in range(max(1, half - 2), half - 1):
                 multiply(-d)
@@ -388,6 +395,12 @@
         return carry
 
     lax.fori_loop(1, plane, stats_send, 0)
+    for copies in ring_copies:
+        for copy in copies[-2:]:
+            copy.wait_send()
+    for copy in sent:
+        copy.wait_send()
+    sent.clear()
     lax.fori_loop(1, plane, stats_wait, 0)
     top_s, top_t = stats[0, 0:1, :], stats[0, 2:3, :]
     for i in range(1, plane):
@@ -568,7 +581,6 @@
     for ox in range(1, 4):
         column_sums[ox] = sum_y(ox)
         two_x[ox] = column_sums[ox].astype(BF16)
-        begin(remote(two_x.at[ox], end_x.at[ox], exs_sem.at[ox], exr_sem.at[ox], in_plane((xi + ox) % 4, yi)))
     second_half = sum_y(0)
     column_sums[0] = second_half
     near_products = [jnp.zeros((half_tok, 128), F32)] * 4
@@ -603,6 +615,8 @@
         return carry
 
     lax.fori_loop(1, plane, told_send, 0)
+    for ox in (2, 1, 3):
+        begin(remote(two_x.at[ox], end_x.at[ox], exs_sem.at[ox], exr_sem.at[ox], in_plane((xi + ox) % 4, yi)))
     heard[me] = close
 
     def slice_sent(i, carry):
@@ -615,12 +629,6 @@
     lax.fori_loop(0, ny, slice_sent, 0)
 
     loss_wait(2)
-    for copies in ring_copies:
-        for copy in copies[-2:]:
-            copy.wait_send()
-    for copy in sent:
-        copy.wait_send()
-    sent.clear()
     for oy in range(1, ny):
         remote(end_y.at[oy], end_y.at[oy], eys_sem.at[oy], eyr_sem.at[oy], mate).wait_recv()
         first_half = first_half + end_y[oy].astype(F32)

time: 98.5 us -> 98.1 us (level)
  no operation moved by 1% of the time
where the time goes in v3:
time: 98.1 us; the launch traced here: 98 us
  Pallas kernels  94.9 us (97%)
  between operations  2.33 us (2%)
    pallas_call x1, Pallas kernels, per_device(): pl.pallas_call(functools.partial(kernel, nz, n_voc), out_shape=(jax.Shape...  94.9 us

profile of v3, /device:TPU:1, one launch (start us, length us, event | category | flops | bytes accessed | tf_op | source)
XLA Modules:
  0.0 98.0 jit_solution(5166144364165887750)
XLA Ops:
  0.6 94.9 %shard_map.86 = (bf16[1,2,2,128,512]{4,3,2,1,0:T(8,128)(2,1)S(1)}, f32[1,1]{1,0:T(1,128)}) custom-call(bf16[2,128,4096]{2,1,0:T(8,128)(2,1)} %hidden.1, bf16[256,1280]{1,0:T(8,128)(2,1)} %head.1, bf16[2,128,1280]{2,1,0:T(8,128)(2,1)} %teacher.1, s32[2,128]{1,0:T(2,128)} %targets.1, bf16[1,2,2,128,512]{4,3,2,1,0:T(8,128)(2,1)} %xin.1, f32[1,2,512]{2,1,0:T(2,128)} %gains.1, ...), custom_call_target="tpu_custom_call" | custom-call | tf_op jit(solution)/shard_map/pallas_call | solution.py:703
  95.5 0.8 copy.11

commit v4 on v3

--- a/solution.py
+++ b/solution.py
@@ -134,8 +134,8 @@
         held = []
         if k > 1:
             held = ring_wait(way, ring_parts[way].index((k - 1, part)))
-        if i >= 2:
-            ring_copies[way][i - 2].wait_send()
+        if i >= 1:
+            ring_copies[way][i - 1].wait_send()
         copy = remote(src, slot, zs_sem.at[way, i], zr_sem.at[way, i], right if way == 0 else left)
         copy.start()
         ring_copies[way].append(copy)
@@ -396,7 +396,7 @@
 
     lax.fori_loop(1, plane, stats_send, 0)
     for copies in ring_copies:
-        for copy in copies[-2:]:
+        for copy in copies[-1:]:
             copy.wait_send()
     for copy in sent:
         copy.wait_send()

time: 98.1 us -> 104 us (1.060)
  Pallas kernels: 94.9 us -> 100 us
    pallas_call x1, Pallas kernels: 94.9 us -> 100 us  [per_device(): pl.pallas_call(functools.partial(kernel, nz, n_voc), out_shape=(jax.Shape...]
where the time goes in v4:
time: 104 us
  Pallas kernels  100 us (96%)
  between operations  2.33 us (2%)
    pallas_call x1, Pallas kernels, per_device(): pl.pallas_call(functools.partial(kernel, nz, n_voc), out_shape=(jax.Shape...  100 us

profile of v4, /device:TPU:1, one launch (start us, length us, event | category | flops | bytes accessed | tf_op | source)
XLA Modules:
  0.0 103.6 jit_solution(891238434546133658)
XLA Ops:
  0.6 100.5 %shard_map.86 = (bf16[1,2,2,128,512]{4,3,2,1,0:T(8,128)(2,1)S(1)}, f32[1,1]{1,0:T(1,128)}) custom-call(bf16[2,128,4096]{2,1,0:T(8,128)(2,1)} %hidden.1, bf16[256,1280]{1,0:T(8,128)(2,1)} %head.1, bf16[2,128,1280]{2,1,0:T(8,128)(2,1)} %teacher.1, s32[2,128]{1,0:T(2,128)} %targets.1, bf16[1,2,2,128,512]{4,3,2,1,0:T(8,128)(2,1)} %xin.1, f32[1,2,512]{2,1,0:T(2,128)} %gains.1, ...), custom_call_target="tpu_custom_call" | custom-call | tf_op jit(solution)/shard_map/pallas_call | solution.py:703
  101.1 0.8 copy.11

commit v5 on v4

--- a/solution.py
+++ b/solution.py
@@ -134,8 +134,8 @@
         held = []
         if k > 1:
             held = ring_wait(way, ring_parts[way].index((k - 1, part)))
-        if i >= 1:
-            ring_copies[way][i - 1].wait_send()
+        if i >= 3:
+            ring_copies[way][i - 3].wait_send()
         copy = remote(src, slot, zs_sem.at[way, i], zr_sem.at[way, i], right if way == 0 else left)
         copy.start()
         ring_copies[way].append(copy)
@@ -396,7 +396,7 @@
 
     lax.fori_loop(1, plane, stats_send, 0)
     for copies in ring_copies:
-        for copy in copies[-1:]:
+        for copy in copies[-3:]:
             copy.wait_send()
     for copy in sent:
         copy.wait_send()

time: 104 us -> 98.1 us (0.943)
  Pallas kernels: 100 us -> 94.9 us
    pallas_call x1, Pallas kernels: 100 us -> 94.9 us  [per_device(): pl.pallas_call(functools.partial(kernel, nz, n_voc), out_shape=(jax.Shape...]
where the time goes in v5:
time: 98.1 us; the launch traced here: 98 us
  Pallas kernels  94.9 us (97%)
  between operations  2.33 us (2%)
    pallas_call x1, Pallas kernels, per_device(): pl.pallas_call(functools.partial(kernel, nz, n_voc), out_shape=(jax.Shape...  94.9 us

profile of v5, /device:TPU:1, one launch (start us, length us, event | category | flops | bytes accessed | tf_op | source)
XLA Modules:
  0.0 98.0 jit_solution(3974918054211243718)
XLA Ops:
  0.6 94.9 %shard_map.86 = (bf16[1,2,2,128,512]{4,3,2,1,0:T(8,128)(2,1)S(1)}, f32[1,1]{1,0:T(1,128)}) custom-call(bf16[2,128,4096]{2,1,0:T(8,128)(2,1)} %hidden.1, bf16[256,1280]{1,0:T(8,128)(2,1)} %head.1, bf16[2,128,1280]{2,1,0:T(8,128)(2,1)} %teacher.1, s32[2,128]{1,0:T(2,128)} %targets.1, bf16[1,2,2,128,512]{4,3,2,1,0:T(8,128)(2,1)} %xin.1, f32[1,2,512]{2,1,0:T(2,128)} %gains.1, ...), custom_call_target="tpu_custom_call" | custom-call | tf_op jit(solution)/shard_map/pallas_call | solution.py:703
  95.5 0.8 copy.11
